TPU v7x, 32 devices: a whole 2x2x4 slice. The times are simulated.
32 devices in a mesh: edp: 8 (over y, x, core), etp: 4 (over z).
Axes of the slice: x: 2, y: 2, z: 4, core: 2. Of those that a mesh axis runs over, the one named last changes fastest.
Arguments:
- tokens: bfloat16 [4096, 3072], P('edp'), may hold values from -6 to 6
- expert_ids: int32 [4096, 2], P('edp'), may hold values from 0 to 7, as said below
- route_weight: float32 [4096, 2], P('edp'), may hold values from 0.2 to 1
- index_list: int32 [8, 256], P('edp'), may hold values from 0 to 512, as said below
- gate_weight: bfloat16 [3072, 8192], P('edp', 'etp'), may hold values from -0.109375 to 0.109375
- up_weight: bfloat16 [3072, 8192], P('edp', 'etp'), may hold values from -0.109375 to 0.109375
- down_weight: bfloat16 [8192, 3072], P('etp', 'edp'), may hold values from -0.0625 to 0.0625
Outputs:
- expert_out: bfloat16 [4096, 3072], P(('edp', 'etp'))
Inputs may be any that keep to these rules, and one draw needn't show every extreme that they name: `index_list`: row b lists, increasing, the positions within block b of the tokens that name expert 0, then 512 in the remaining slots; in every draw some block is full. `expert_ids`: each token names two different experts; a token names expert 0 exactly when its position stands in its block's row of index_list.
All inputs are finite; a program needn't handle non-finite values.
Results may differ from a plain program's by a relative error of at most 0.018.
Values may be sent and summed in bfloat16 or wider, within the bound.
A program may use at most 128 MiB of HBM per device.

v0:
```python
import jax
import jax.numpy as jnp
from jax import lax
from jax.sharding import PartitionSpec as P


def shards(tokens, expert_ids, route_weight, index_list, gate_weight, up_weight, down_weight):
    block_rows = tokens.shape[0]
    slot_rows = index_list[0]
    combine = jnp.sum(
        jnp.where(expert_ids == 0, route_weight, jnp.zeros_like(route_weight)), axis=1
    )
    is_live = slot_rows < block_rows
    safe_rows = jnp.minimum(slot_rows, block_rows - 1)
    inputs = jnp.take(tokens, safe_rows, axis=0)
    row_scale = jnp.where(is_live, jnp.take(combine, safe_rows), jnp.zeros_like(combine[:1]))
    gate_next = jnp.dot(
        inputs,
        lax.all_gather(gate_weight, "edp", axis=0, tiled=True),
        preferred_element_type=jnp.float32,
    )
    up_next = jnp.dot(
        inputs,
        lax.all_gather(up_weight, "edp", axis=0, tiled=True),
        preferred_element_type=jnp.float32,
    )
    hidden = (jax.nn.silu(gate_next) * up_next * row_scale[:, None]).astype(jnp.bfloat16)
    partial_terms = jnp.dot(
        hidden,
        lax.all_gather(down_weight, "edp", axis=1, tiled=True),
        preferred_element_type=jnp.float32,
    )
    placing = (jnp.arange(block_rows)[:, None] == slot_rows[None, :]).astype(jnp.float32)
    partial_terms = jnp.dot(placing, partial_terms, preferred_element_type=jnp.float32)
    shares = lax.psum_scatter(
        partial_terms.astype(jnp.bfloat16), "etp", scatter_dimension=0, tiled=True
    )
    return shares


def solution(mesh):
    in_specs = (
        P("edp", None),
        P("edp", None),
        P("edp", None),
        P("edp", None),
        P("edp", "etp"),
        P("edp", "etp"),
        P("etp", "edp"),
    )
    out_specs = P(("edp", "etp"), None)
    return jax.shard_map(shards, mesh=mesh, in_specs=in_specs, out_specs=out_specs, check_vma=False)
```

profile of v0, /device:TPU:0, one launch (start us, length us, event | category | flops | bytes accessed | tf_op | source)
XLA Modules:
  0.0 312.3 jit_solution(12373573609725879040)
XLA Ops:
  6.5 0.0 copy-start
  6.5 0.0 copy-start.1
  6.5 0.0 all-gather.4.cloned.1.call-start
  6.5 0.7 all-gather.4.cloned.1.call-update
  7.3 0.0 all-gather.6.cloned.1.call-start
  7.3 0.7 all-gather.6.cloned.1.call-update
  8.0 0.0 all-gather.8.cloned.1.call-start
  8.1 0.7 all-gather.8.cloned.1.call-update
  8.7 0.0 reduce-scatter.2.cloned.1.call-start
  8.8 0.0 copy-done.1
  8.8 0.0 copy-done
  8.8 0.0 copy-start.2
  8.8 0.0 copy-start.3
  8.9 2.7 gather_fusion
  11.5 0.0 copy-done.2
  11.6 0.0 copy-done.3
  11.6 1.9 gather_fusion.1
  13.6 70.6 %all-gather.4.cloned.1.call-done = bf16[3072,2048]{1,0:T(8,128)(2,1)} async-done(((bf16[384,2048]{1,0:T(8,128)(2,1)}), bf16[3072,2048]{1,0:T(8,128)(2,1)}) %all-gather.4.cloned.1.call-update) | async-done | bytes 12582928 | tf_op jit(solution)/shard_map/all_gather | solution.py:19
  84.1 9.8 %fusion.4 = f32[256,2048]{1,0:T(8,128)} fusion(bf16[3072,2048]{1,0:T(8,128)(2,1)} %all-gather.4.cloned.1.call-done, bf16[256,3072]{1,0:T(8,128)(2,1)} %gather_fusion, pred[256]{0:T(512)(128)(4,1)S(1)} %compare_and_fusion), kind=kOutput, calls=%fused_computation.8 | convolution fusion | flops 3222011904 | bytes 16253184 | tf_op jit(solution)/shard_map/dot_general | solution.py:17
  93.9 64.2 %all-gather.6.cloned.1.call-done = bf16[3072,2048]{1,0:T(8,128)(2,1)} async-done(((bf16[384,2048]{1,0:T(8,128)(2,1)}), bf16[3072,2048]{1,0:T(8,128)(2,1)}) %all-gather.6.cloned.1.call-update) | async-done | bytes 12582928 | tf_op jit(solution)/shard_map/all_gather | solution.py:24
  158.2 10.3 %fusion.1 = bf16[256,2048]{1,0:T(8,128)(2,1)} fusion(bf16[3072,2048]{1,0:T(8,128)(2,1)} %all-gather.6.cloned.1.call-done, f32[256,2048]{1,0:T(8,128)} %fusion.4, f32[256]{0:T(256)S(1)} %compare_select_fusion.3, bf16[256,3072]{1,0:T(8,128)(2,1)} %gather_fusion, pred[256]{0:T(512)(128)(4,1)S(1)} %compare_and_fusion), kind=kOutput, calls=%fused_computation.5 | convolution fusion | flops 3225681920 | bytes 17302784 | tf_op jit(solution)/shard_map/dot_general | solution.py:22
  168.5 66.1 %all-gather.8.cloned.1.call-done = bf16[2048,3072]{1,0:T(8,128)(2,1)} async-done(((bf16[2048,384]{1,0:T(8,128)(2,1)}), bf16[2048,3072]{1,0:T(8,128)(2,1)}) %all-gather.8.cloned.1.call-update) | async-done | bytes 12582928 | tf_op jit(solution)/shard_map/all_gather | solution.py:30
  234.6 10.8 %convolution_convert_fusion = bf16[512,3072]{1,0:T(8,128)(2,1)} fusion(bf16[256,2048]{1,0:T(8,128)(2,1)} %fusion.1, bf16[2048,3072]{1,0:T(8,128)(2,1)} %all-gather.8.cloned.1.call-done, s32[256]{0:T(256)S(1)} %bitcast.10), kind=kOutput, calls=%fused_computation.2 | convolution fusion | flops 4028235776 | bytes 16778240 | tf_op jit(solution)/shard_map/dot_general | solution.py:34
  245.4 0.0 reduce-scatter.2.cloned.1.call-update
  245.4 60.4 %reduce-scatter.2.cloned.1.call-done = bf16[128,3072]{1,0:T(8,128)(2,1)} async-done(((bf16[512,3072]{1,0:T(8,128)(2,1)}), bf16[128,3072]{1,0:T(8,128)(2,1)}) %reduce-scatter.2.cloned.1.call-update) | async-done | bytes 786448 | tf_op jit(solution)/shard_map/reduce_scatter | solution.py:35
  (5 shorter events, 0.0 us)
Async XLA Ops:
  6.5 2.3 copy-start
  6.5 2.3 copy-start.1
  6.5 77.6 %all-gather.4.cloned.1.call-start = ((), (), s32[]{:S(2)}) async-start(), calls=%async_computation.1 | async-start | bytes 14155776 | tf_op jit(solution)/shard_map/all_gather | solution.py:19
  7.3 150.9 %all-gather.6.cloned.1.call-start = ((), (), s32[]{:S(2)}) async-start(), calls=%async_computation.2 | async-start | bytes 14155776 | tf_op jit(solution)/shard_map/all_gather | solution.py:24
  8.0 226.6 %all-gather.8.cloned.1.call-start = ((), (), s32[]{:S(2)}) async-start(), calls=%async_computation.3 | async-start | bytes 14155776 | tf_op jit(solution)/shard_map/all_gather | solution.py:30
  8.7 297.1 %reduce-scatter.2.cloned.1.call-start = ((), (), s32[]{:S(2)}) async-start(), calls=%async_computation.4 | async-start | bytes 3932160 | tf_op jit(solution)/shard_map/reduce_scatter | solution.py:35
  8.8 2.7 copy-start.2
  8.8 2.7 copy-start.3
Sparse Core Ops, SparseCore 0:
  9.3 74.8 all-gather.3
  86.0 72.1 all-gather.5
  160.0 74.5 all-gather.7
  245.5 60.2 reduce-scatter.1
where the time goes:
time: 312 us
  waiting for transfers between devices  263 us (84%)
  matrix products  30.9 us (10%)
  between operations  13.2 us (4%)
  local copies, waits for them, and re-layouts  4.66 us (1%)
    all_gather x1, waiting for transfers between devices, shards(): lax.all_gather(gate_weight, 'edp', axis=0, tiled=True)  70.6 us
    all_gather x1, waiting for transfers between devices, shards(): lax.all_gather(down_weight, 'edp', axis=1, tiled=True)  66.1 us
    all_gather x1, waiting for transfers between devices, shards(): lax.all_gather(up_weight, 'edp', axis=0, tiled=True)  64.2 us
    reduce_scatter x1, waiting for transfers between devices, shards(): lax.psum_scatter(partial_terms.astype(jnp.bfloat16), 'etp', scatter_dimen...  60.4 us
    dot_general x1, matrix products, shards(): jnp.dot(placing, partial_terms, preferred_element_type=jnp.float32)  10.8 us
    dot_general x1, matrix products, shards(): jnp.dot(inputs, lax.all_gather(up_weight, 'edp', axis=0, tiled=True), pre...  10.3 us
    dot_general x1, matrix products, shards(): jnp.dot(inputs, lax.all_gather(gate_weight, 'edp', axis=0, tiled=True), p...  9.82 us
  transfers between devices with their start and end apart: 4, of which 4 were waited for; matrix products, arithmetic and copies ran while one was open for 8% of the time, Pallas kernels for 0%

commit v1 on v0

v1 whole, which is shorter than its diff:
```python
import functools

import jax
import jax.numpy as jnp
from jax import lax
from jax.experimental import pallas as pl
from jax.experimental.pallas import tpu as pltpu
from jax.sharding import PartitionSpec as P

MESH = pl.DeviceIdType.MESH
BF16 = jnp.bfloat16
F32 = jnp.float32


def dot(a, b):
    return jnp.dot(a, b, preferred_element_type=F32)


def kernel(
    n, ranks, parts,
    gate_hbm, up_hbm, down_hbm, tok_hbm, idx_row, idx_col, comb,
    out_ref,
    tok, x_own, x_other, x_send, w_gate, w_up, down, part_send, part_recv, part_own, hidden, placing, z_send, z_recv,
    tok_sem, x_sems, w_recv, w_sib, w_far, p_send, p_recv, d_recv, d_sib, d_far, d_fwd, s_send, s_recv,
):
    e = lax.axis_index("edp")
    t = lax.axis_index("etp")
    group = n // 2
    chips = group // 2
    h, g = e // group, e % group
    q, c = g // 2, g % 2
    rows, width = gate_hbm.shape
    cols = down_hbm.shape[1]
    slots = idx_col.shape[0]
    depth = group * rows
    piece = width // parts

    def at(hh, qq, cc):
        return hh * group + qq * 2 + cc

    sibling = (at(h, q, 1 - c), t)
    partner = (at(1 - h, q, c), t)

    def far(k):
        return (q + k) % chips

    def remote(src, dst, send, recv, dev):
        return pltpu.make_async_remote_copy(
            src_ref=src, dst_ref=dst, send_sem=send, recv_sem=recv, device_id=dev, device_id_type=MESH
        )

    barrier = pltpu.get_barrier_semaphore()
    pl.semaphore_signal(barrier, inc=1, device_id=sibling, device_id_type=MESH)

    @pl.loop(1, 2 * chips)
    def _(m):
        dev = (at((h + m // chips) % 2, (q + m % chips) % chips, c), t)
        pl.semaphore_signal(barrier, inc=1, device_id=dev, device_id_type=MESH)

    @pl.loop(1, ranks)
    def _(k):
        pl.semaphore_signal(barrier, inc=1, device_id=(e, (t + k) % ranks), device_id_type=MESH)

    tok_copy = pltpu.make_async_copy(tok_hbm, tok, tok_sem)
    tok_copy.start()
    pl.semaphore_wait(barrier, 2 * chips + ranks - 1)

    weights = ((gate_hbm, w_gate), (up_hbm, w_up))

    def w_src(i, f):
        return weights[i][0].at[:, pl.ds(f * piece, piece)]

    def w_dst(i, f, gg):
        return weights[i][1].at[pl.ds(pl.multiple_of(gg * rows, 32), rows), pl.ds(f * piece, piece)]

    def w_far_copy(i, f, k):
        return remote(w_src(i, f), w_dst(i, f, g), w_far.at[f, i, k - 1], w_recv.at[f, i, g], (at(h, far(k), c), t))

    def w_local(i, f):
        return pltpu.make_async_copy(w_src(i, f), w_dst(i, f, g), w_recv.at[f, i, g])

    def w_own_sib(i, f):
        return remote(w_src(i, f), w_dst(i, f, g), w_sib.at[f, i, 0], w_recv.at[f, i, g], sibling)

    def w_relay(i, f, k):
        gg = far(k) * 2 + c
        return remote(w_dst(i, f, gg), w_dst(i, f, gg), w_sib.at[f, i, k], w_recv.at[f, i, gg], sibling)

    def w_arrived(i, f, gg):
        ref = w_dst(i, f, gg)
        remote(ref, ref, w_sib.at[f, i, 0], w_recv.at[f, i, gg], sibling).wait_recv()

    def start_far(f):
        for i in range(2):
            for k in range(1, chips):
                w_far_copy(i, f, k).start()

    def start_near(f):
        for i in range(2):
            w_local(i, f).start()
            w_own_sib(i, f).start()

    start_far(0)
    start_near(0)
    if parts > 1:
        start_far(1)

    tok_copy.wait()
    tokens_in = tok.shape[0]
    hit = lax.broadcasted_iota(jnp.int32, (slots, tokens_in), 1) == idx_col[...]
    scale = jnp.sum(jnp.where(hit, comb[...], 0.0), axis=1, keepdims=True)
    pick = hit.astype(F32).astype(BF16)
    mine = pl.ds(pl.multiple_of(h * depth, 128), depth)
    theirs = pl.ds(pl.multiple_of((1 - h) * depth, 128), depth)
    x_send[...] = dot(pick, tok[:, theirs]).astype(BF16)
    x_copy = remote(x_send, x_other, x_sems.at[0], x_sems.at[1], partner)
    x_copy.start()
    x_own[...] = dot(pick, tok[:, mine]).astype(BF16)
    placing[...] = (
        lax.broadcasted_iota(jnp.int32, (tokens_in, slots), 0) == idx_row[...]
    ).astype(F32).astype(BF16)
    for f in range(1, parts):
        start_near(f)

    def part_copy(i, f):
        span = pl.ds(f * piece, piece)
        return remote(part_send.at[i, :, span], part_recv.at[i, :, span], p_send.at[f, i], p_recv.at[f, i], partner)

    def gather(f):
        for i in range(2):
            for k in range(1, chips):
                w_arrived(i, f, far(k) * 2 + c)
                w_relay(i, f, k).start()
        if f + 2 < parts:
            for i in range(2):
                for k in range(1, chips):
                    w_far_copy(i, f, k).wait_send()
            start_far(f + 2)
        if f == 0:
            x_copy.wait_recv()
        for i in range(2):
            w_local(i, f).wait()
            w_arrived(i, f, q * 2 + 1 - c)
            for k in range(1, chips):
                w_arrived(i, f, far(k) * 2 + 1 - c)
            wref = weights[i][1]
            tile = min(piece, 256)

            @pl.loop(0, piece // tile)
            def _(m):
                span = pl.ds(pl.multiple_of(f * piece + m * tile, 128), tile)
                part_send[i, :, span] = dot(x_other[...], wref[:, span]).astype(BF16)

            part_copy(i, f).start()

            @pl.loop(0, piece // tile)
            def _(m):
                span = pl.ds(pl.multiple_of(f * piece + m * tile, 128), tile)
                part_own[i, :, span] = dot(x_own[...], wref[:, span])

    def activate(f):
        for i in range(2):
            part_copy(i, f).wait_recv()
        span = pl.ds(f * piece, piece)
        gate = part_own[0, :, span] + part_recv[0, :, span].astype(F32)
        up = part_own[1, :, span] + part_recv[1, :, span].astype(F32)
        hidden[:, span] = (gate / (1.0 + jnp.exp(-gate)) * up * scale).astype(BF16)

    def d_own(dev, sem):
        return remote(down_hbm, down.at[e], sem, d_recv.at[e], dev)

    def d_far_copy(k):
        return d_own((at(h, far(k), c), t), d_far.at[k])

    def d_local():
        return pltpu.make_async_copy(down_hbm, down.at[e], d_recv.at[e])

    def d_relay(m, s):
        return remote(down.at[s], down.at[s], d_sib.at[m], d_recv.at[s], sibling)

    def d_arrived(s):
        remote(down.at[s], down.at[s], d_sib.at[0], d_recv.at[s], sibling).wait_recv()

    def forward(k):
        s = jnp.where(c == 0, at(h, far(k), c), at(1 - h, q, c))
        dev = jnp.where(c == 0, at(1 - h, q, c), at(h, far(k), c))
        return remote(down.at[s], down.at[s], d_fwd.at[k - 1], d_recv.at[s], (dev, t))

    def start_down():
        for k in range(1, chips):
            d_far_copy(k).start()
        d_local().start()
        d_own(sibling, d_sib.at[0]).start()

    for f in range(parts):
        gather(f)
        if f == parts - 1:
            start_down()
            d_own(partner, d_far.at[0]).start()
        if f >= 1:
            activate(f - 1)
    activate(parts - 1)

    def z_copy(s, k):
        peer = (t + k) % ranks
        return remote(z_send.at[s, peer], z_recv.at[s, t], s_send.at[s, peer], s_recv.at[s, t], (e, peer))

    def share(s):
        part = dot(hidden[...], down[s]).astype(BF16)
        placed = dot(placing[...], part).astype(BF16)
        z_send[s] = placed.reshape(ranks, tokens_in // ranks, cols)

        @pl.loop(1, ranks)
        def _(k):
            z_copy(s, k).start()

    d_local().wait()
    share(e)
    near = at(h, q, 1 - c)
    d_arrived(near)
    share(near)

    @pl.loop(1, 2 * chips)
    def _(m):
        hh, qq = (h + m // chips) % 2, (q + m % chips) % chips
        s = at(hh, qq, c)
        d_arrived(s)

        @pl.when(jnp.logical_and(c == 0, m < chips))
        def _():
            remote(down.at[s], down.at[s], d_fwd.at[m - 1], d_recv.at[s], partner).start()

        @pl.when(jnp.logical_and(c == 1, m == chips))
        def _():
            for k in range(1, chips):
                remote(down.at[s], down.at[s], d_fwd.at[k - 1], d_recv.at[s], (at(h, far(k), c), t)).start()

        d_relay(m, s).start()
        share(s)
        other = at(hh, qq, 1 - c)
        d_arrived(other)
        share(other)

    @pl.loop(0, n)
    def _(s):
        total = z_send[s, t].astype(F32)
        for k in range(1, ranks):
            src = (t + k) % ranks
            remote(z_send.at[s, src], z_recv.at[s, src], s_send.at[s, src], s_recv.at[s, src], (e, src)).wait_recv()
            total = total + z_recv[s, src].astype(F32)
        out_ref[s] = total.astype(BF16)

    x_copy.wait_send()
    for f in range(parts):
        for i in range(2):
            w_own_sib(i, f).wait_send()
            part_copy(i, f).wait_send()
            for k in range(1, chips):
                w_relay(i, f, k).wait_send()
                if f + 2 >= parts:
                    w_far_copy(i, f, k).wait_send()
    d_own(sibling, d_sib.at[0]).wait_send()
    d_own(partner, d_far.at[0]).wait_send()
    for k in range(1, chips):
        d_far_copy(k).wait_send()
        forward(k).wait_send()

    @pl.loop(1, 2 * chips)
    def _(m):
        d_relay(m, at((h + m // chips) % 2, (q + m % chips) % chips, c)).wait_send()

    @pl.loop(0, n)
    def _(s):
        @pl.loop(1, ranks)
        def _(k):
            z_copy(s, k).wait_send()


def shards(n, ranks, tokens, expert_ids, route_weight, index_list, gate_weight, up_weight, down_weight):
    tokens_in, model = tokens.shape
    slots = index_list.shape[1]
    rows, width = gate_weight.shape
    cols = down_weight.shape[1]
    group = n // 2
    chips = group // 2
    depth = group * rows
    parts = 4
    combine = jnp.sum(jnp.where(expert_ids == 0, route_weight, jnp.zeros_like(route_weight)), axis=1)
    share = tokens_in // ranks
    hbm = pl.BlockSpec(memory_space=pl.ANY)
    vmem = pl.BlockSpec(memory_space=pltpu.VMEM)
    dma = pltpu.SemaphoreType.DMA
    out = pl.pallas_call(
        functools.partial(kernel, n, ranks, parts),
        out_shape=jax.ShapeDtypeStruct((n, share, cols), BF16),
        in_specs=[hbm, hbm, hbm, hbm, vmem, vmem, vmem],
        out_specs=vmem,
        scratch_shapes=[
            pltpu.VMEM((tokens_in, model), BF16),
            pltpu.VMEM((slots, depth), BF16),
            pltpu.VMEM((slots, depth), BF16),
            pltpu.VMEM((slots, depth), BF16),
            pltpu.VMEM((depth, width), BF16),
            pltpu.VMEM((depth, width), BF16),
            pltpu.VMEM((n, width, cols), BF16),
            pltpu.VMEM((2, slots, width), BF16),
            pltpu.VMEM((2, slots, width), BF16),
            pltpu.VMEM((2, slots, width), F32),
            pltpu.VMEM((slots, width), BF16),
            pltpu.VMEM((tokens_in, slots), BF16),
            pltpu.VMEM((n, ranks, share, cols), BF16),
            pltpu.VMEM((n, ranks, share, cols), BF16),
            dma,
            dma((2,)),
            dma((parts, 2, group)),
            dma((parts, 2, chips)),
            dma((parts, 2, chips)),
            dma((parts, 2)),
            dma((parts, 2)),
            dma((n,)),
            dma((2 * chips,)),
            dma((chips,)),
            dma((chips,)),
            dma((n, ranks)),
            dma((n, ranks)),
        ],
        compiler_params=pltpu.CompilerParams(
            collective_id=0, has_side_effects=True, vmem_limit_bytes=60 * 1024 * 1024
        ),
        cost_estimate=pl.CostEstimate(
            flops=2 * slots * model * width * 3, bytes_accessed=3 * n * rows * width * 2, transcendentals=slots * width
        ),
    )(
        gate_weight, up_weight, down_weight, tokens,
        index_list, index_list.reshape(slots, 1), combine.reshape(1, tokens_in),
    )
    return out.transpose(1, 0, 2).reshape(share, model)


def solution(mesh):
    in_specs = (
        P("edp", None),
        P("edp", None),
        P("edp", None),
        P("edp", None),
        P("edp", "etp"),
        P("edp", "etp"),
        P("etp", "edp"),
    )
    out_specs = P(("edp", "etp"), None)
    body = functools.partial(shards, mesh.shape["edp"], mesh.shape["etp"])
    return jax.shard_map(body, mesh=mesh, in_specs=in_specs, out_specs=out_specs, check_vma=False)
```

time: 312 us -> 175 us (0.56)
  waiting for transfers between devices: 263 us -> 0 us
  Pallas kernels: 0 us -> 169 us
  matrix products: 30.9 us -> 0 us
  between operations: 13.2 us -> 0.02 us
    all_gather x3 -> x0, waiting for transfers between devices: 201 us -> none  [the longest x1 70.6 us: shards(): lax.all_gather(gate_weight, 'edp', axis=0, tiled=True)]
    pallas_call x0 -> x1, Pallas kernels: none -> 169 us  [shards(): pl.pallas_call(functools.partial(kernel, n, ranks, parts), out_shape=jax....]
    reduce_scatter x1 -> x0, waiting for transfers between devices: 60.4 us -> none  [shards(): lax.psum_scatter(partial_terms.astype(jnp.bfloat16), 'etp', scatter_dimen...]
    dot_general x3 -> x0, matrix products: 30.9 us -> none  [the longest x1 10.8 us: shards(): jnp.dot(placing, partial_terms, preferred_element_type=jnp.float32)]
    gather x2 -> x0, local copies, waits for them, and re-layouts: 4.63 us -> none  [the longest x1 2.69 us: shards(): inputs = jnp.take(tokens, safe_rows, axis=0)]
  transfers between devices with their start and end apart: 4 -> 0, of which waited for: 4 -> 0; matrix products, arithmetic and copies ran while one was open for 8% -> 0% of each run, Pallas kernels for 0% -> 0%
where the time goes in v1:
time: 175 us
  Pallas kernels  169 us (97%)
  local copies, waits for them, and re-layouts  4.14 us (2%)
    pallas_call x1, Pallas kernels, shards(): pl.pallas_call(functools.partial(kernel, n, ranks, parts), out_shape=jax....  169 us

profile of v1, /device:TPU:0, one launch (start us, length us, event | category | flops | bytes accessed | tf_op | source)
XLA Modules:
  0.0 174.7 jit_solution(7560212862797046464)
XLA Ops:
  0.0 1.3 fusion
  1.3 1.5 copy.8.idx_col
  2.8 169.2 %shard_map.73 = bf16[8,128,384]{2,1,0:T(8,128)(2,1)} custom-call(bf16[384,2048]{1,0:T(8,128)(2,1)} %gate_hbm.1, bf16[384,2048]{1,0:T(8,128)(2,1)} %up_hbm.1, bf16[2048,384]{1,0:T(8,128)(2,1)} %down_hbm.1, bf16[512,3072]{1,0:T(8,128)(2,1)} %tok_hbm.1, s32[1,256]{1,0:T(1,128)} %idx_row.1, s32[256,1]{1,0:T(8,128)} %copy.8.idx_col, f32[1,512]{1,0:T(1,128)} %bitcast.6), custom_call_target="tpu_custom_call" | custom-call | flops 9663676416 | bytes 37748736 | tf_op jit(solution)/shard_map/pallas_call | solution.py:293
  172.0 1.5 copy.9
  173.5 1.2 copy.10

commit v2 on v1

--- a/solution.py
+++ b/solution.py
@@ -131,6 +131,8 @@
             for k in range(1, chips):
                 w_arrived(i, f, far(k) * 2 + c)
                 w_relay(i, f, k).start()
+        if f == parts - 1:
+            start_down()
         if f + 2 < parts:
             for i in range(2):
                 for k in range(1, chips):
@@ -195,7 +197,6 @@
     for f in range(parts):
         gather(f)
         if f == parts - 1:
-            start_down()
             d_own(partner, d_far.at[0]).start()
         if f >= 1:
             activate(f - 1)
@@ -284,7 +285,7 @@
     group = n // 2
     chips = group // 2
     depth = group * rows
-    parts = 4
+    parts = max(1, width // 256)
     combine = jnp.sum(jnp.where(expert_ids == 0, route_weight, jnp.zeros_like(route_weight)), axis=1)
     share = tokens_in // ranks
     hbm = pl.BlockSpec(memory_space=pl.ANY)

time: 175 us -> 170 us (0.971)
  Pallas kernels: 169 us -> 164 us
    pallas_call x1, Pallas kernels: 169 us -> 164 us  [shards(): pl.pallas_call(functools.partial(kernel, n, ranks, parts), out_shape=jax....]
where the time goes in v2:
time: 170 us
  Pallas kernels  164 us (96%)
  local copies, waits for them, and re-layouts  4.14 us (2%)
    pallas_call x1, Pallas kernels, shards(): pl.pallas_call(functools.partial(kernel, n, ranks, parts), out_shape=jax....  164 us

profile of v2, /device:TPU:0, one launch (start us, length us, event | category | flops | bytes accessed | tf_op | source)
XLA Modules:
  0.0 169.9 jit_solution(13335688244303343428)
XLA Ops:
  0.0 1.3 fusion
  1.3 1.5 copy.8.idx_col
  2.8 164.4 %shard_map.73 = bf16[8,128,384]{2,1,0:T(8,128)(2,1)} custom-call(bf16[384,2048]{1,0:T(8,128)(2,1)} %gate_hbm.1, bf16[384,2048]{1,0:T(8,128)(2,1)} %up_hbm.1, bf16[2048,384]{1,0:T(8,128)(2,1)} %down_hbm.1, bf16[512,3072]{1,0:T(8,128)(2,1)} %tok_hbm.1, s32[1,256]{1,0:T(1,128)} %idx_row.1, s32[256,1]{1,0:T(8,128)} %copy.8.idx_col, f32[1,512]{1,0:T(1,128)} %bitcast.6), custom_call_target="tpu_custom_call" | custom-call | flops 9663676416 | bytes 37748736 | tf_op jit(solution)/shard_map/pallas_call | solution.py:294
  167.2 1.5 copy.9
  168.7 1.2 copy.10
